TPU v7x, 32 devices: a whole 2x2x4 slice. The times are simulated.
32 devices in a mesh: groups: 2 (over x), lon: 16 (over z, y, core).
Axes of the slice: x: 2, y: 2, z: 4, core: 2. Of those that a mesh axis runs over, the one named last changes fastest.
Arguments:
- queries: bfloat16 [8192, 1024], P(('groups', 'lon')), parts along dimension 0, may hold values from -8 to 8
- key_tokens: bfloat16 [8192, 1024], P(('groups', 'lon')), parts along dimension 0, may hold values from -8 to 8
- value_tokens: bfloat16 [8192, 1024], P(('groups', 'lon')), parts along dimension 0, may hold values from -6 to 6
- grad_out: bfloat16 [8192, 1024], P(('groups', 'lon')), parts along dimension 0, may hold values from -6 to 6
- out_weight: bfloat16 [1024, 1024], replicated, may hold values from -3 to 3
- pattern: int32 [32, 3], replicated, may hold values from 0 to 31, as said below
- valid_rows: int32 [32], replicated, may hold values from 64 to 128, as said below
Outputs:
- layer_out: bfloat16 [8192, 1024], P(('groups', 'lon')), parts along dimension 0
- grad_queries: bfloat16 [8192, 1024], P(('groups', 'lon')), parts along dimension 0
- grad_keys: bfloat16 [8192, 1024], P(('groups', 'lon')), parts along dimension 0
- grad_values: bfloat16 [8192, 1024], P(('groups', 'lon')), parts along dimension 0
There are 2 independent parts, one for each index of `groups`. A program takes and returns all parts, laid end to end along the dimension named above; an argument that names none is the same for every part. Nothing has to cross between parts.
Inputs may be any that keep to these rules, and one draw needn't show every extreme that they name: `pattern`: block g lies in longitude strip g // 2 at latitude index g % 2. Row g names three key blocks: column 1 is g itself, column 0 a block of strip (g // 2 - 1) mod 16, column 2 a block of strip (g // 2 + 1) mod 16, each at a latitude index that differs from g's by at most one. The first valid_rows[g] tokens of block g are live, the others are padding.
All inputs are finite; a program needn't handle non-finite values.
Results may differ from a plain program's by a relative error of at most 0.028.
Values may be sent and summed in bfloat16 or wider, within the bound.
A program may use at most 128 MiB of HBM per device.

v0:
```python
import jax
import jax.numpy as jnp
from jax import lax
from jax.sharding import PartitionSpec as P

HEADS = 16
TILE = 128


def with_halo(cells, sides, width):
    for axis, dim in sides:
        count = lax.axis_size(axis)
        head = lax.slice_in_dim(cells, 0, width, axis=dim)
        tail = lax.slice_in_dim(cells, cells.shape[dim] - width, cells.shape[dim], axis=dim)
        cells = jnp.concatenate(
            [
                lax.ppermute(tail, axis, [(i, (i + 1) % count) for i in range(count)]),
                cells,
                lax.ppermute(head, axis, [((i + 1) % count, i) for i in range(count)]),
            ],
            axis=dim,
        )
    return cells


def passed_along(block, axis, distance):
    devices = range(lax.axis_size(axis))
    route = [((i - distance) % len(devices), i) for i in devices]
    return lax.ppermute(block, axis, route)


def split_heads(tensor):
    return tensor.reshape(tensor.shape[:-1] + (HEADS, tensor.shape[-1] // HEADS))


def live_rows(counts):
    return jnp.arange(TILE, dtype=jnp.int32)[None, :] < counts[:, None]


def per_device(queries, key_tokens, value_tokens, grad_out, out_weight, pattern, valid_rows):
    strip_count = lax.axis_size("lon")
    position = lax.axis_index("lon")
    row_count, features = queries.shape
    blocks = row_count // TILE
    score_scale = (features // HEADS) ** (-0.5)
    near_span = 3 * TILE
    strips = (position + jnp.arange(3, dtype=jnp.int32) - 1) % strip_count
    near_counts = jnp.stack(
        [
            lax.dynamic_slice_in_dim(valid_rows, strips[offset] * blocks, blocks, 0)
            for offset in range(3)
        ]
    )
    near_pattern = jnp.stack(
        [
            lax.dynamic_slice_in_dim(pattern, strips[offset] * blocks, blocks, 0)
            for offset in range(3)
        ]
    )
    near_live = live_rows(near_counts.reshape(-1)).reshape(3, blocks, TILE)
    own_live = near_live[1]
    root_counts = jnp.sqrt(near_counts[1].astype(jnp.float32))
    picked = jnp.arange(3, dtype=jnp.int32)[None, :] * blocks + near_pattern[1] % blocks
    key_value = jnp.stack((key_tokens, value_tokens))
    bordered = with_halo(key_value, (("lon", 1),), row_count)
    bordered = bordered.reshape(2, 3 * blocks, TILE, features)
    pooled = jnp.einsum(
        "gt,xgtd->xgd",
        own_live.astype(jnp.bfloat16),
        key_value.reshape(2, blocks, TILE, features),
        preferred_element_type=jnp.float32,
    )
    summary = (pooled / root_counts[None, :, None]).astype(jnp.bfloat16)
    summaries = lax.all_gather(summary, "lon", axis=1, tiled=True)
    far_keys = split_heads(summaries[0])
    far_values = split_heads(summaries[1])
    far_count = summaries.shape[1]
    near_pairs = bordered[:, picked].reshape(2, blocks, near_span, features)
    near_keys = split_heads(near_pairs[0])
    near_values = split_heads(near_pairs[1])
    near_mask = near_live.reshape(3 * blocks, TILE)[picked].reshape(blocks, near_span)
    query_heads = split_heads(queries.reshape(blocks, TILE, features))
    near_scores = (
        jnp.einsum("bthc,blhc->bhtl", query_heads, near_keys, preferred_element_type=jnp.float32)
        * score_scale
    )
    near_scores = jnp.where(near_mask[:, None, None, :], near_scores, -jnp.inf)
    far_scores = (
        jnp.einsum("bthc,shc->bhts", query_heads, far_keys, preferred_element_type=jnp.float32)
        * score_scale
    )
    row_top = jnp.maximum(jnp.max(near_scores, axis=-1), jnp.max(far_scores, axis=-1))
    total = jnp.sum(jnp.exp(near_scores - row_top[..., None]), axis=-1) + jnp.sum(
        jnp.exp(far_scores - row_top[..., None]), axis=-1
    )
    log_total = row_top + jnp.log(total)
    near_chances = jnp.exp(near_scores - log_total[..., None])
    far_chances = jnp.exp(far_scores - log_total[..., None])
    near_rounded = near_chances.astype(jnp.bfloat16)
    far_rounded = far_chances.astype(jnp.bfloat16)
    mixed_heads = jnp.einsum(
        "bhtl,blhc->bthc", near_rounded, near_values, preferred_element_type=jnp.float32
    )
    mixed_heads = mixed_heads + jnp.einsum(
        "bhts,shc->bthc", far_rounded, far_values, preferred_element_type=jnp.float32
    )
    attended = mixed_heads.astype(jnp.bfloat16)
    layer_out = jnp.dot(
        attended.reshape(row_count, features), out_weight, preferred_element_type=jnp.float32
    ).astype(jnp.bfloat16)
    grad_attended = lax.dot_general(
        grad_out, out_weight, (((1,), (1,)), ((), ())), preferred_element_type=jnp.float32
    ).astype(jnp.bfloat16)
    grad_heads = split_heads(grad_attended.reshape(blocks, TILE, features))
    row_delta = jnp.einsum(
        "bthc,bthc->bht", grad_heads, attended, preferred_element_type=jnp.float32
    )
    near_grad_chances = jnp.einsum(
        "bthc,blhc->bhtl", grad_heads, near_values, preferred_element_type=jnp.float32
    )
    far_grad_chances = jnp.einsum(
        "bthc,shc->bhts", grad_heads, far_values, preferred_element_type=jnp.float32
    )
    near_grad_scores = (
        near_chances * (near_grad_chances - row_delta[..., None]) * score_scale
    ).astype(jnp.bfloat16)
    far_grad_scores = (
        far_chances * (far_grad_chances - row_delta[..., None]) * score_scale
    ).astype(jnp.bfloat16)
    grad_query = jnp.einsum(
        "bhtl,blhc->bthc", near_grad_scores, near_keys, preferred_element_type=jnp.float32
    )
    grad_query = grad_query + jnp.einsum(
        "bhts,shc->bthc", far_grad_scores, far_keys, preferred_element_type=jnp.float32
    )
    grad_queries = grad_query.astype(jnp.bfloat16).reshape(row_count, features)
    far_grad_keys = jnp.einsum(
        "bhts,bthc->shc", far_grad_scores, query_heads, preferred_element_type=jnp.float32
    ).reshape(far_count, features)
    far_grad_values = jnp.einsum(
        "bhts,bthc->shc", far_rounded, grad_heads, preferred_element_type=jnp.float32
    ).reshape(far_count, features)
    far_grads = lax.psum_scatter(
        jnp.stack((far_grad_keys, far_grad_values)), "lon", scatter_dimension=1, tiled=True
    )
    spread = (
        own_live.astype(jnp.float32)[None, :, :, None]
        * (far_grads / root_counts[None, :, None])[:, :, None, :]
    )
    spread = spread.reshape(2, row_count, features)
    near_grad_keys = jnp.einsum(
        "bhtl,bthc->blhc", near_grad_scores, query_heads, preferred_element_type=jnp.float32
    )
    near_grad_values = jnp.einsum(
        "bhtl,bthc->blhc", near_rounded, grad_heads, preferred_element_type=jnp.float32
    )
    onehot = (
        picked.reshape(-1)[:, None] == jnp.arange(3 * blocks, dtype=jnp.int32)[None, :]
    ).astype(jnp.float32)
    stacked = jnp.stack((near_grad_keys, near_grad_values)).reshape(2, 3 * blocks, TILE * features)
    placed = jnp.einsum("ne,xnk->xek", onehot, stacked, precision=lax.Precision.HIGHEST).reshape(
        2, 3, row_count, features
    )
    from_east = passed_along(placed[:, 0].astype(jnp.bfloat16), "lon", -1).astype(jnp.float32)
    from_west = passed_along(placed[:, 2].astype(jnp.bfloat16), "lon", 1).astype(jnp.float32)
    gathered = placed[:, 1] + from_east + from_west
    totals = gathered + spread
    return (layer_out, grad_queries, totals[0].astype(jnp.bfloat16), totals[1].astype(jnp.bfloat16))


def solution(mesh):
    return jax.shard_map(
        per_device,
        mesh=mesh,
        in_specs=(
            P(("groups", "lon"), None),
            P(("groups", "lon"), None),
            P(("groups", "lon"), None),
            P(("groups", "lon"), None),
            P(),
            P(),
            P(),
        ),
        out_specs=(
            P(("groups", "lon"), None),
            P(("groups", "lon"), None),
            P(("groups", "lon"), None),
            P(("groups", "lon"), None),
        ),
        check_vma=False,
    )
```

profile of v0, /device:TPU:0, one launch (start us, length us, event | category | flops | bytes accessed | tf_op | source)
XLA Modules:
  0.0 214.0 jit_solution(10437834198670715514)
XLA Ops:
  7.2 2.4 %pad_maximum_fusion.1 = bf16[2,256,1024]{2,1,0:T(8,128)(2,1)} fusion(bf16[1,256,1024]{2,1,0:T(8,128)(2,1)} %bitcast.169, bf16[1,256,1024]{2,1,0:T(8,128)(2,1)} %bitcast.172), kind=kLoop, calls=%fused_computation.45 | loop fusion | flops 524288 | bytes 2097152 | tf_op jit(solution)/shard_map/stack | solution.py:64
  9.7 5.4 %collective-permute-start.1 = (bf16[2,256,1024]{2,1,0:T(8,128)(2,1)}, bf16[2,256,1024]{2,1,0:T(8,128)(2,1)}, u32[]{:S(2)}, u32[]{:S(2)}) collective-permute-start(bf16[2,256,1024]{2,1,0:T(8,128)(2,1)} %pad_maximum_fusion.1), channel_id=1, source_target_pairs={{1,0},{2,1},{3,2},{4,3},{5,4},{6,5},{7,6},{8,7},{9,8},{10,9},{11,1... | collective-permute-start | bytes 3145736 | tf_op jit(solution)/shard_map/ppermute | solution.py:19
  15.1 0.6 fusion.63
  17.7 0.7 convert_sqrt_fusion
  18.4 0.8 dynamic-slice_bitcast_fusion.1
  19.5 0.5 fusion.54
  20.0 0.8 compare_select_fusion
  20.9 1.4 fusion.20
  22.6 0.7 eq.19
  23.2 0.6 gather_fusion.1
  23.8 25.8 %all_gather.3 = bf16[2,32,1024]{2,0,1:T(2,128)(2,1)S(1)} all-gather(bf16[2,2,1024]{2,0,1:T(2,128)(2,1)S(1)} %fusion.47), channel_id=1, replica_groups=mesh['groups'=2,'lon'=16] {'lon'}, dimensions={1}, use_global_device_ids=true | all-gather | bytes 139264 | tf_op jit(solution)/shard_map/all_gather | solution.py:74
  49.6 0.5 slice_reduce_fusion
  50.1 0.1 reshape_squeeze.15
  50.3 0.1 reshape_squeeze.14
  50.4 0.2 copy.110
  50.8 2.6 %convolution_convert_fusion = bf16[256,1024]{1,0:T(8,128)(2,1)} fusion(bf16[256,1024]{1,0:T(8,128)(2,1)} %param.10, bf16[1024,1024]{1,0:T(8,128)(2,1)S(1)} %copy-done), kind=kOutput, calls=%fused_computation.30 | convolution fusion | flops 537133056 | bytes 3145728 | tf_op jit(solution)/shard_map/dot_general | solution.py:111
  53.4 1.2 copy.122
  54.6 0.9 reshape_reshape.7
  55.6 0.6 dynamic-slice
  56.8 0.2 fusion.64
  57.0 2.4 %bitcast_convert_fusion = f32[2,16,128,64]{2,0,3,1:T(2,128)} fusion(bf16[2,128,16,64]{1,0,3,2:T(2,128)(2,1)} %reshape_reshape.7), kind=kLoop, calls=%fused_computation.54 | loop fusion | flops 262144 | bytes 1572864
  59.5 3.4 %pad_maximum_fusion = bf16[2,768,1024]{2,1,0:T(8,128)(2,1)} fusion(bf16[2,256,1024]{2,1,0:T(8,128)(2,1)} %collective-permute-done.1, bf16[1,256,1024]{2,1,0:T(8,128)(2,1)} %bitcast.171, bf16[1,256,1024]{2,1,0:T(8,128)(2,1)} %bitcast.174, bf16[2,256,1024]{2,1,0:T(8,128)(2,1)} %collective-permute-done), kind=kLoop, calls=%fused_computation.15 | loop fusion | flops 12582912 | bytes 6291456 | tf_op jit(solution)/shard_map/concatenate | solution.py:15
  62.9 4.4 %gather_fusion = bf16[6,2,128,1024]{3,2,1,0:T(8,128)(2,1)} fusion(bf16[2,6,128,1024]{3,2,1,0:T(8,128)(2,1)} %bitcast.168, s32[1024]{0:T(1024)S(1)} %pad_clamp_fusion), kind=kCustom, calls=%fused_computation | custom fusion | bytes 6291480 | tf_op jit(solution)/shard_map/gather | solution.py:78
  67.3 3.8 %fusion.62 = (bf16[1,2,3,128,1024]{4,3,0,2,1:T(8,128)(2,1)}, bf16[1,2,3,128,1024]{4,3,0,2,1:T(8,128)(2,1)}) fusion(bf16[2,2,3,128,1024]{4,3,0,2,1:T(8,128)(2,1)} %bitcast.167), kind=kLoop, calls=%fused_computation.116 | loop fusion | bytes 6291456 | tf_op jit(solution)/shard_map/slice | solution.py:80
  71.1 4.2 %copy.108 = bf16[1,2,3,128,1024]{3,2,4,1,0:T(4,128)(2,1)} copy(bf16[1,2,3,128,1024]{4,3,0,2,1:T(8,128)(2,1)} %get-tuple-element.22) | data formatting | bytes 3145728 | tf_op jit(solution)/shard_map/slice | solution.py:80
  75.3 5.1 %reshape_squeeze.12 = bf16[2,384,16,64]{1,3,2,0:T(8,128)(2,1)} reshape(bf16[1,2,3,128,1024]{3,2,4,1,0:T(4,128)(2,1)} %copy.108) | data formatting | bytes 3145728 | tf_op jit(solution)/shard_map/reshape;squeeze | solution.py:33
  80.4 4.2 %copy.109 = bf16[1,2,3,128,1024]{3,2,4,1,0:T(4,128)(2,1)} copy(bf16[1,2,3,128,1024]{4,3,0,2,1:T(8,128)(2,1)} %get-tuple-element.23) | data formatting | bytes 3145728 | tf_op jit(solution)/shard_map/slice | solution.py:79
  84.6 5.1 %reshape_squeeze.13 = bf16[2,384,16,64]{1,3,2,0:T(8,128)(2,1)} reshape(bf16[1,2,3,128,1024]{3,2,4,1,0:T(4,128)(2,1)} %copy.109) | data formatting | bytes 3145728 | tf_op jit(solution)/shard_map/reshape;squeeze | solution.py:33
  89.7 3.0 %bitcast_reduce_fusion = (f32[2,16,128]{2,1,0:T(8,128)S(1)}, f32[2,16,384,128]{3,2,1,0:T(8,128)S(1)}) fusion(pred[2,384]{1,0:T(4,128)(4,1)S(1)} %broadcast_in_dim.17, bf16[2,384,16,64]{1,3,2,0:T(8,128)(2,1)} %reshape_squeeze.13, bf16[2,128,16,64]{1,0,3,2:T(2,128)(2,1)S(1)} %reshape_reshape.6), kind=kOutput, calls=%fused_computation.8 | convolution fusion | flops 206041088 | bytes 8405760 | tf_op jit(solution)/shard_map/bthc,blhc->bhtl/dot_general | solution.py:84
  92.7 1.4 fusion.4
  94.4 0.3 convolution_bitcast_fusion.8
  94.7 0.4 convolution_bitcast_fusion.4
  95.0 0.6 copy-done.5
  95.6 0.3 copy-done.7
  95.9 2.6 %multiply_reduce_fusion = (f32[2,16,128]{2,1,0:T(8,128)S(1)}, bf16[2,128,16,64]{1,3,2,0:T(8,128)(2,1)}) fusion(f32[2,16,128,64]{2,0,3,1:T(2,128)S(1)} %copy-done.7, f32[2,128,16,64]{1,3,2,0:T(8,128)S(1)} %convolution_bitcast_fusion.4, bf16[2,384,16,64]{1,3,2,0:T(8,128)(2,1)S(1)} %copy-done.5, f32[2,16,384,128]{3,2,1,0:T(8,128)S(1)} %get-tuple-element.35, ...), kind=kOutput, calls=%fused_computation.47 | convolution fusion | flops 208924672 | bytes 10519296 | tf_op jit(solution)/shard_map/bhtl,blhc->bthc/dot_general | solution.py:101
  98.5 0.6 copy.128
  99.1 3.9 %multiply_convert_fusion = bf16[2,16,128,384]{2,3,1,0:T(8,128)(2,1)} fusion(f32[2,16,384,128]{3,2,1,0:T(8,128)S(1)} %get-tuple-element.35, f32[2,16,128]{2,1,0:T(8,128)S(1)} %get-tuple-element.38, f32[2,16,128]{2,1,0:T(8,128)S(1)} %fusion.45, pred[2,384]{1,0:T(4,128)(4,1)S(1)} %broadcast_in_dim.17, bf16[2,384,16,64]{1,3,2,0:T(8,128)(2,1)S(1)} %copy-done.5, ...), kind=kOutput, calls=%fused_computation.12 | convolution fusion | flops 212336640 | bytes 11567872 | tf_op jit(solution)/shard_map/bthc,blhc->bhtl/dot_general | solution.py:118
  103.0 3.2 %convolution_bitcast_fusion.1 = f32[2,384,16,64]{1,3,2,0:T(8,128)} fusion(bf16[2,128,16,64]{1,0,3,2:T(2,128)(2,1)S(1)} %copy-done.2, f32[2,16,384,128]{3,2,1,0:T(8,128)S(1)} %get-tuple-element.35, f32[2,16,128]{2,1,0:T(8,128)S(1)} %fusion.45, pred[2,384]{1,0:T(4,128)(4,1)S(1)} %broadcast_in_dim.17), kind=kOutput, calls=%fused_computation.22 | convolution fusion | flops 207618048 | bytes 9978624 | tf_op jit(solution)/shard_map/bhtl,bthc->blhc/dot_general | solution.py:154
  106.3 0.2 copy.144
  106.4 0.8 stack_reshape.7
  107.2 2.4 %copy.121 = bf16[2,128,16,64]{1,0,3,2:T(2,128)(2,1)} copy(bf16[2,128,16,64]{1,3,2,0:T(8,128)(2,1)} %get-tuple-element.39) | data formatting | bytes 1048576 | tf_op jit(solution)/shard_map/convert_element_type | solution.py:107
  109.6 1.3 fusion.19
  110.9 0.3 convolution_bitcast_fusion.9
  111.1 0.2 copy.142
  111.4 1.6 pad_maximum_fusion.3
  113.1 5.1 %convolution_bitcast_fusion.2 = f32[2,384,16,64]{1,3,2,0:T(8,128)} fusion(bf16[2,16,128,384]{2,3,1,0:T(8,128)(2,1)} %multiply_convert_fusion, bf16[2,128,16,64]{1,0,3,2:T(2,128)(2,1)S(1)} %reshape_reshape.6), kind=kOutput, calls=%fused_computation.23 | convolution fusion | flops 201326592 | bytes 6815744 | tf_op jit(solution)/shard_map/bhtl,bthc->blhc/dot_general | solution.py:151
  118.2 6.1 %copy.134 = f32[2,384,16,64]{3,2,1,0:T(8,128)} copy(f32[2,384,16,64]{1,3,2,0:T(8,128)} %convolution_bitcast_fusion.2) | data formatting | bytes 6291456 | tf_op jit(solution)/shard_map/bhtl,bthc->blhc/transpose | solution.py:151
  124.3 6.6 %stack.49 = f32[1,6,131072]{2,1,0:T(8,128)} reshape(f32[2,384,16,64]{3,2,1,0:T(8,128)} %copy.134) | data formatting | bytes 6291456 | tf_op jit(solution)/shard_map/stack | solution.py:160
  130.9 6.1 %copy.137 = f32[2,384,16,64]{3,2,1,0:T(8,128)} copy(f32[2,384,16,64]{1,3,2,0:T(8,128)} %convolution_bitcast_fusion.1) | data formatting | bytes 6291456 | tf_op jit(solution)/shard_map/bhtl,bthc->blhc/transpose | solution.py:154
  137.0 6.6 %stack.50 = f32[1,6,131072]{2,1,0:T(8,128)} reshape(f32[2,384,16,64]{3,2,1,0:T(8,128)} %copy.137) | data formatting | bytes 6291456 | tf_op jit(solution)/shard_map/stack | solution.py:160
  143.7 11.1 %convolution_bitcast_fusion = f32[2,6,131072]{2,1,0:T(8,128)} fusion(f32[1,6,131072]{2,1,0:T(8,128)} %stack.50, f32[1,6,131072]{2,1,0:T(8,128)} %stack.49, s32[6]{0:T(128)S(1)} %copy-done.12), kind=kOutput, calls=%fused_computation.2 | convolution fusion | flops 114819104 | bytes 12582936 | tf_op jit(solution)/shard_map/ne,xnk->xek/dot_general | solution.py:161
  154.8 7.2 %reshape.84 = f32[2,3,256,1024]{3,2,1,0:T(8,128)} reshape(f32[2,6,131072]{2,1,0:T(8,128)} %convolution_bitcast_fusion) | data formatting | bytes 12582912 | tf_op jit(solution)/shard_map/reshape | solution.py:161
  161.9 3.3 %convert.9 = bf16[2,3,256,1024]{3,2,1,0:T(8,128)(2,1)S(1)} convert(f32[2,3,256,1024]{3,2,1,0:T(8,128)} %reshape.84) | non-fusion elementwise | flops 1572864 | bytes 9437184 | tf_op jit(solution)/shard_map/convert.4
  165.2 1.5 slice_bitcast_fusion.2
  166.7 1.4 collective-permute-start.2
  168.2 0.3 convolution_bitcast_fusion.3
  168.5 1.5 fusion.14
  170.1 1.5 convolution_convert_fusion.1
  171.6 1.8 copy.168
  173.5 1.5 reshape.119
  175.0 27.4 %all-reduce.3.cloned.1.call-done = f32[2,32,1024]{2,1,0:T(8,128)} async-done(((f32[2,32,1024]{2,1,0:T(8,128)}), f32[2,32,1024]{2,1,0:T(8,128)}) %all-reduce.3.cloned.1.call-update) | async-done | bytes 262160
  202.4 0.9 dynamic-slice_divide_fusion
  203.3 2.8 %fusion.10 = bf16[2,256,1024]{2,1,0:T(8,128)(2,1)S(1)} fusion(f32[2,3,256,1024]{3,2,1,0:T(8,128)} %reshape.84, bf16[2,256,1024]{2,1,0:T(8,128)(2,1)} %collective-permute-done.3, bf16[2,256,1024]{2,1,0:T(8,128)(2,1)} %collective-permute-done.2, f32[2,2,1024]{2,1,0:T(2,128)S(1)} %dynamic-slice_divide_fusion, f32[256]{0:T(256)S(1)} %copy-done.9), kind=kLoop, calls=%fused_computation.20 | loop fusion | flops 3670016 | bytes 5260288 | tf_op jit(solution)/shard_map/convert.2
  206.1 1.0 slice_bitcast_fusion.3
  (52 shorter events, 1.1 us)
Async XLA Ops:
  7.2 43.6 %copy-start = (bf16[1024,1024]{1,0:T(8,128)(2,1)S(1)}, bf16[1024,1024]{1,0:T(8,128)(2,1)}, u32[]{:S(2)}) copy-start(bf16[1024,1024]{1,0:T(8,128)(2,1)} %param.11) | copy-start | bytes 6291460
  7.2 43.3 %copy-start.8 = (bf16[256,1024]{1,0:T(8,128)(2,1)S(1)}, bf16[256,1024]{1,0:T(8,128)(2,1)}, u32[]{:S(2)}) copy-start(bf16[256,1024]{1,0:T(8,128)(2,1)} %param.7) | copy-start | bytes 1572868
  7.2 195.2 %all-reduce.3.cloned.1.call-start = ((), (), s32[]{:S(2)}) async-start(), calls=%async_computation | async-start | bytes 524288
  9.7 49.8 %collective-permute-start.1 = (bf16[2,256,1024]{2,1,0:T(8,128)(2,1)}, bf16[2,256,1024]{2,1,0:T(8,128)(2,1)}, u32[]{:S(2)}, u32[]{:S(2)}) collective-permute-start(bf16[2,256,1024]{2,1,0:T(8,128)(2,1)} %pad_maximum_fusion.1), channel_id=1, source_target_pairs={{1,0},{2,1},{3,2},{4,3},{5,4},{6,5},{7,6},{8,7},{9,8},{10,9},{11,1... | collective-permute-start | bytes 3145736 | tf_op jit(solution)/shard_map/ppermute | solution.py:19
  15.1 44.3 %collective-permute-start = (bf16[2,256,1024]{2,1,0:T(8,128)(2,1)}, bf16[2,256,1024]{2,1,0:T(8,128)(2,1)}, u32[]{:S(2)}, u32[]{:S(2)}) collective-permute-start(bf16[2,256,1024]{2,1,0:T(8,128)(2,1)} %pad_maximum_fusion.1), channel_id=1, source_target_pairs={{0,1},{1,2},{2,3},{3,4},{4,5},{5,6},{6,7},{7,8},{8,9},{9,10},{10,1... | collective-permute-start | bytes 3145736 | tf_op jit(solution)/shard_map/ppermute | solution.py:17
  18.4 5.4 %copy-start.10 = (f32[2]{0:T(128)}, f32[2]{0:T(128)S(1)}, u32[]{:S(2)}) copy-start(f32[2]{0:T(128)S(1)} %convert_sqrt_fusion) | copy-start | bytes 28
  50.3 44.4 %copy-start.6 = (bf16[32,16,64]{2,1,0:T(8,128)(2,1)}, bf16[32,16,64]{2,1,0:T(8,128)(2,1)S(1)}, u32[]{:S(2)}) copy-start(bf16[32,16,64]{2,1,0:T(8,128)(2,1)S(1)} %reshape_squeeze.15) | copy-start | bytes 196612
  50.6 4.9 %copy-start.13 = (u32[32]{0:T(128)S(1)}, u32[32]{0:T(128)}, u32[]{:S(2)}) copy-start(u32[32]{0:T(128)} %constant.57) | copy-start | bytes 388
  92.7 1.6 copy-start.2
  94.2 1.4 copy-start.5
  94.2 1.7 copy-start.7
  137.0 6.6 %copy-start.12 = (s32[6]{0:T(128)S(1)}, s32[6]{0:T(128)}, u32[]{:S(2)}) copy-start(s32[6]{0:T(128)} %eq.19) | copy-start | bytes 76
  165.2 3.3 %copy-start.1 = (bf16[2,384,16,64]{1,3,2,0:T(8,128)(2,1)S(1)}, bf16[2,384,16,64]{1,3,2,0:T(8,128)(2,1)}, u32[]{:S(2)}) copy-start(bf16[2,384,16,64]{1,3,2,0:T(8,128)(2,1)} %reshape_squeeze.13) | copy-start | bytes 4718596
  165.2 3.3 %copy-start.3 = (bf16[2,16,128,384]{2,3,1,0:T(8,128)(2,1)S(1)}, bf16[2,16,128,384]{2,3,1,0:T(8,128)(2,1)}, u32[]{:S(2)}) copy-start(bf16[2,16,128,384]{2,3,1,0:T(8,128)(2,1)} %multiply_convert_fusion) | copy-start | bytes 9437188
  166.7 36.6 %collective-permute-start.2 = (bf16[2,256,1024]{2,1,0:T(8,128)(2,1)}, bf16[2,256,1024]{2,1,0:T(8,128)(2,1)}, u32[]{:S(2)}, u32[]{:S(2)}) collective-permute-start(bf16[2,256,1024]{2,1,0:T(8,128)(2,1)} %get-tuple-element.20), channel_id=1, source_target_pairs={{1,0},{2,1},{3,2},{4,3},{5,4},{6,5},{7,6},{8,7},{9,8},{10,9},{11,1... | collective-permute-start | bytes 3145736 | tf_op jit(solution)/shard_map/ppermute | solution.py:29
  168.2 35.1 %collective-permute-start.3 = (bf16[2,256,1024]{2,1,0:T(8,128)(2,1)}, bf16[2,256,1024]{2,1,0:T(8,128)(2,1)}, u32[]{:S(2)}, u32[]{:S(2)}) collective-permute-start(bf16[2,256,1024]{2,1,0:T(8,128)(2,1)} %get-tuple-element.21), channel_id=1, source_target_pairs={{15,0},{0,1},{1,2},{2,3},{3,4},{4,5},{5,6},{6,7},{7,8},{8,9},{9,10... | collective-permute-start | bytes 3145736 | tf_op jit(solution)/shard_map/ppermute | solution.py:29
  168.5 1.6 copy-start.4
  170.1 32.3 %copy-start.11 = (f32[2]{0:T(128)S(1)}, f32[2]{0:T(128)}, u32[]{:S(2)}) copy-start(f32[2]{0:T(128)} %copy-done.10) | copy-start | bytes 28
  170.1 33.2 %copy-start.9 = (f32[256]{0:T(256)S(1)}, f32[256]{0:T(256)}, u32[]{:S(2)}) copy-start(f32[256]{0:T(256)} %get-tuple-element.26) | copy-start | bytes 3076
Sparse Core Ops, SparseCore 0:
  113.2 89.1 all-reduce.2
where the time goes:
time: 215 us; the launch traced here: 214 us
  local copies, waits for them, and re-layouts  77.4 us (36%)
  matrix products  38.8 us (18%)
  waiting for transfers between devices  27.4 us (13%)
  blocking collectives  25.8 us (12%)
  other arithmetic  20.7 us (10%)
  between operations  16.9 us (8%)
  starting transfers between devices  6.92 us (3%)
    unnamed x2, waiting for transfers between devices  27.4 us
    all_gather x1, blocking collectives, per_device(): summaries = lax.all_gather(summary, 'lon', axis=1, tiled=True)  25.8 us
    another operation x2, local copies, waits for them, and re-layouts, per_device(): jnp.stack((near_grad_keys, near_grad_values))  13.3 us
    another operation x6, local copies, waits for them, and re-layouts, split_heads(): tensor.reshape(tensor.shape[:-1] + (HEADS, tensor.shape[-1] // HEADS))  11.6 us
    dot_general x1, matrix products, per_device(): jnp.einsum('ne,xnk->xek', onehot, stacked, precision=lax.Precision.HIGHEST)  11.1 us
    slice x2, local copies, waits for them, and re-layouts, per_device(): near_values = split_heads(near_pairs[1])  7.98 us
    reshape x1, local copies, waits for them, and re-layouts, per_device(): jnp.einsum('ne,xnk->xek', onehot, stacked, precision=lax.Precision.HIGHEST)  7.16 us
    transpose x1, local copies, waits for them, and re-layouts, per_device(): jnp.einsum('bhtl,bthc->blhc', near_grad_scores, query_heads, preferred_el...  6.11 us
  transfers between devices with their start and end apart: 5, of which 1 were waited for; matrix products, arithmetic and copies ran while one was open for 36% of the time, Pallas kernels for 0%

commit v1 on v0

--- a/solution.py
+++ b/solution.py
@@ -5,6 +5,33 @@
 
 HEADS = 16
 TILE = 128
+
+
+def create_limits(inputs, pos_dim):
+    inputs = jnp.moveaxis(inputs, 0, pos_dim)
+    t_next = inputs.shape
+    return inputs.reshape(
+        *t_next[:pos_dim], t_next[pos_dim] * t_next[pos_dim + 1], *t_next[pos_dim + 2 :]
+    )
+
+
+def _use_pieces_all(x0, ax_name):
+    z2, block_out = (lax.axis_size(ax_name), lax.axis_index(ax_name))
+    local_out, prior = (x0[None], 1)
+    while prior < z2:
+        mid_arr = lax.ppermute(
+            local_out, ax_name, list(map(lambda ii: (ii, ii ^ prior), range(z2)))
+        )
+        reached = block_out & prior == 0
+        local_out = jnp.concatenate(
+            [jnp.where(reached, local_out, mid_arr), jnp.where(reached, mid_arr, local_out)]
+        )
+        prior *= 2
+    return local_out
+
+
+def ranges_number(local_x, at_axis, own_rows):
+    return create_limits(_use_pieces_all(own_rows, local_x), at_axis)
 
 
 def with_halo(cells, sides, width):
@@ -71,7 +98,7 @@
         preferred_element_type=jnp.float32,
     )
     summary = (pooled / root_counts[None, :, None]).astype(jnp.bfloat16)
-    summaries = lax.all_gather(summary, "lon", axis=1, tiled=True)
+    summaries = ranges_number("lon", 1, summary)
     far_keys = split_heads(summaries[0])
     far_values = split_heads(summaries[1])
     far_count = summaries.shape[1]

time: 215 us -> 207 us (0.963)
  blocking collectives: 25.8 us -> 0 us
  waiting for transfers between devices: 27.4 us -> 41.9 us
  starting transfers between devices: 6.92 us -> 11.6 us
    all_gather x1 -> x0, blocking collectives: 25.8 us -> none  [per_device(): summaries = lax.all_gather(summary, 'lon', axis=1, tiled=True)]
    ppermute x0 -> x4, waiting for transfers between devices: none -> 14.2 us  [_use_pieces_all(): lax.ppermute(local_out, ax_name, list(map(lambda ii: (ii, ii ^ prior), ra...]
    ppermute x0 -> x4, starting transfers between devices: none -> 4.44 us  [_use_pieces_all(): lax.ppermute(local_out, ax_name, list(map(lambda ii: (ii, ii ^ prior), ra...]
    unnamed x32 -> x40, local copies, waits for them, and re-layouts: 5.05 us -> 6.91 us
  transfers between devices with their start and end apart: 5 -> 9, of which waited for: 1 -> 3; matrix products, arithmetic and copies ran while one was open for 36% -> 37% of each run, Pallas kernels for 0% -> 0%
where the time goes in v1:
time: 207 us; the launch traced here: 205 us
  local copies, waits for them, and re-layouts  78 us (38%)
  waiting for transfers between devices  41.9 us (20%)
  matrix products  37 us (18%)
  other arithmetic  19.8 us (10%)
  between operations  17.1 us (8%)
  starting transfers between devices  11.6 us (6%)
    unnamed x2, waiting for transfers between devices  27.7 us
    ppermute x4, waiting for transfers between devices, _use_pieces_all(): lax.ppermute(local_out, ax_name, list(map(lambda ii: (ii, ii ^ prior), ra...  14.2 us
    another operation x2, local copies, waits for them, and re-layouts, per_device(): jnp.stack((near_grad_keys, near_grad_values))  13.3 us
    another operation x6, local copies, waits for them, and re-layouts, split_heads(): tensor.reshape(tensor.shape[:-1] + (HEADS, tensor.shape[-1] // HEADS))  11.8 us
    dot_general x1, matrix products, per_device(): jnp.einsum('ne,xnk->xek', onehot, stacked, precision=lax.Precision.HIGHEST)  11.1 us
    slice x2, local copies, waits for them, and re-layouts, per_device(): near_values = split_heads(near_pairs[1])  8.02 us
    reshape x1, local copies, waits for them, and re-layouts, per_device(): jnp.einsum('ne,xnk->xek', onehot, stacked, precision=lax.Precision.HIGHEST)  7.17 us
    unnamed x40, local copies, waits for them, and re-layouts  6.91 us
  transfers between devices with their start and end apart: 9, of which 3 were waited for; matrix products, arithmetic and copies ran while one was open for 37% of the time, Pallas kernels for 0%

profile of v1, /device:TPU:0, one launch (start us, length us, event | category | flops | bytes accessed | tf_op | source)
XLA Modules:
  0.0 205.4 jit_solution(11455381619119806778)
XLA Ops:
  7.2 2.5 %pad_maximum_fusion.1 = bf16[2,256,1024]{2,1,0:T(8,128)(2,1)} fusion(bf16[1,256,1024]{2,1,0:T(8,128)(2,1)} %bitcast.177, bf16[1,256,1024]{2,1,0:T(8,128)(2,1)} %bitcast.180), kind=kLoop, calls=%fused_computation.45 | loop fusion | flops 524288 | bytes 2097152 | tf_op jit(solution)/shard_map/stack | solution.py:91
  9.7 5.4 %collective-permute-start.1 = (bf16[2,256,1024]{2,1,0:T(8,128)(2,1)}, bf16[2,256,1024]{2,1,0:T(8,128)(2,1)}, u32[]{:S(2)}, u32[]{:S(2)}) collective-permute-start(bf16[2,256,1024]{2,1,0:T(8,128)(2,1)} %pad_maximum_fusion.1), channel_id=1, source_target_pairs={{1,0},{2,1},{3,2},{4,3},{5,4},{6,5},{7,6},{8,7},{9,8},{10,9},{11,1... | collective-permute-start | bytes 3145736 | tf_op jit(solution)/shard_map/ppermute | solution.py:46
  15.2 0.6 fusion.64
  17.7 0.7 convert_sqrt_fusion
  18.5 0.8 dynamic-slice_bitcast_fusion.1
  19.5 0.6 fusion.54
  20.1 1.4 fusion.20
  21.7 0.7 convolution_convert_fusion
  22.5 0.2 copy.122
  22.8 1.4 bitcast_convert_fusion
  24.5 12.8 %collective-permute-done.3 = bf16[2,2,2,1024]{3,2,0,1:T(2,128)(2,1)S(1)} collective-permute-done((bf16[2,2,2,1024]{3,2,0,1:T(2,128)(2,1)S(1)}, bf16[2,2,2,1024]{3,2,0,1:T(2,128)(2,1)S(1)}, u32[]{:S(2)}, u32[]{:S(2)}) %collective-permute-start.3) | collective-permute-done | bytes 16416 | tf_op jit(solution)/shard_map/ppermute | solution.py:22
  37.3 1.6 collective-permute-start.4
  39.3 0.6 eq.35
  39.9 1.4 collective-permute-done.4
  41.5 2.7 %collective-permute-start.5 = (bf16[8,2,2,1024]{3,2,0,1:T(2,128)(2,1)S(1)}, bf16[8,2,2,1024]{3,2,0,1:T(2,128)(2,1)S(1)}, u32[]{:S(2)}, u32[]{:S(2)}) collective-permute-start(bf16[8,2,2,1024]{3,2,0,1:T(2,128)(2,1)S(1)} %pad_maximum_fusion.4), channel_id=1, source_target_pairs={{0,8},{1,9},{2,10},{3,11},{4,12},{5,13},{6,14},{7,15},{8,0},{9,1},... | collective-permute-start | bytes 196616 | tf_op jit(solution)/shard_map/ppermute | solution.py:22
  44.2 0.6 gather_fusion.1
  44.7 2.0 copy.110
  46.8 1.2 reshape_reshape.6
  48.0 0.6 dynamic-slice
  49.4 0.2 maximum_bitcast_fusion
  50.0 0.2 fusion.65
  50.2 3.4 %pad_maximum_fusion = bf16[2,768,1024]{2,1,0:T(8,128)(2,1)} fusion(bf16[2,256,1024]{2,1,0:T(8,128)(2,1)} %collective-permute-done.1, bf16[1,256,1024]{2,1,0:T(8,128)(2,1)} %bitcast.179, bf16[1,256,1024]{2,1,0:T(8,128)(2,1)} %bitcast.182, bf16[2,256,1024]{2,1,0:T(8,128)(2,1)} %collective-permute-done), kind=kLoop, calls=%fused_computation.15 | loop fusion | flops 12582912 | bytes 6291456 | tf_op jit(solution)/shard_map/concatenate | solution.py:42
  53.6 4.4 %gather_fusion = bf16[6,2,128,1024]{3,2,1,0:T(8,128)(2,1)} fusion(bf16[2,6,128,1024]{3,2,1,0:T(8,128)(2,1)} %bitcast.176, s32[1024]{0:T(1024)S(1)} %pad_clamp_fusion), kind=kCustom, calls=%fused_computation | custom fusion | bytes 6291480 | tf_op jit(solution)/shard_map/gather | solution.py:105
  58.0 3.9 %fusion.62 = (bf16[1,2,3,128,1024]{4,3,0,2,1:T(8,128)(2,1)}, bf16[1,2,3,128,1024]{4,3,0,2,1:T(8,128)(2,1)}) fusion(bf16[2,2,3,128,1024]{4,3,0,2,1:T(8,128)(2,1)} %bitcast.175), kind=kLoop, calls=%fused_computation.126 | loop fusion | bytes 6291456 | tf_op jit(solution)/shard_map/slice | solution.py:107
  61.9 4.1 %copy.108 = bf16[1,2,3,128,1024]{3,2,4,1,0:T(4,128)(2,1)} copy(bf16[1,2,3,128,1024]{4,3,0,2,1:T(8,128)(2,1)} %get-tuple-element.20) | data formatting | bytes 3145728 | tf_op jit(solution)/shard_map/slice | solution.py:107
  66.1 5.1 %reshape_squeeze.12 = bf16[2,384,16,64]{1,3,2,0:T(8,128)(2,1)} reshape(bf16[1,2,3,128,1024]{3,2,4,1,0:T(4,128)(2,1)} %copy.108) | data formatting | bytes 3145728 | tf_op jit(solution)/shard_map/reshape;squeeze | solution.py:60
  71.2 4.1 %copy.109 = bf16[1,2,3,128,1024]{3,2,4,1,0:T(4,128)(2,1)} copy(bf16[1,2,3,128,1024]{4,3,0,2,1:T(8,128)(2,1)} %get-tuple-element.21) | data formatting | bytes 3145728 | tf_op jit(solution)/shard_map/slice | solution.py:106
  75.3 5.1 %reshape_squeeze.13 = bf16[2,384,16,64]{1,3,2,0:T(8,128)(2,1)} reshape(bf16[1,2,3,128,1024]{3,2,4,1,0:T(4,128)(2,1)} %copy.109) | data formatting | bytes 3145728 | tf_op jit(solution)/shard_map/reshape;squeeze | solution.py:60
  80.5 3.0 %bitcast_reduce_fusion = (f32[2,16,128]{2,1,0:T(8,128)S(1)}, f32[2,16,384,128]{3,2,1,0:T(8,128)S(1)}) fusion(pred[2,384]{1,0:T(4,128)(4,1)S(1)} %broadcast_in_dim.19, bf16[2,384,16,64]{1,3,2,0:T(8,128)(2,1)} %reshape_squeeze.13, bf16[2,128,16,64]{1,0,3,2:T(2,128)(2,1)S(1)} %reshape_reshape.6), kind=kOutput, calls=%fused_computation.8 | convolution fusion | flops 206041088 | bytes 8405760 | tf_op jit(solution)/shard_map/bthc,blhc->bhtl/dot_general | solution.py:111
  83.5 1.4 fusion.4
  85.2 0.3 convolution_bitcast_fusion.8
  85.5 0.4 convolution_bitcast_fusion.4
  85.8 0.6 copy-done.6
  86.4 0.3 copy-done.8
  86.7 2.6 %multiply_reduce_fusion = (f32[2,16,128]{2,1,0:T(8,128)S(1)}, bf16[2,128,16,64]{1,3,2,0:T(8,128)(2,1)}) fusion(f32[2,16,128,64]{2,0,3,1:T(2,128)S(1)} %copy-done.8, f32[2,128,16,64]{1,3,2,0:T(8,128)S(1)} %convolution_bitcast_fusion.4, bf16[2,384,16,64]{1,3,2,0:T(8,128)(2,1)S(1)} %copy-done.6, f32[2,16,384,128]{3,2,1,0:T(8,128)S(1)} %get-tuple-element.43, ...), kind=kOutput, calls=%fused_computation.47 | convolution fusion | flops 208924672 | bytes 10519296 | tf_op jit(solution)/shard_map/bhtl,blhc->bthc/dot_general | solution.py:128
  89.3 0.6 copy.128
  89.9 3.9 %multiply_convert_fusion = bf16[2,16,128,384]{2,3,1,0:T(8,128)(2,1)} fusion(f32[2,16,384,128]{3,2,1,0:T(8,128)S(1)} %get-tuple-element.43, f32[2,16,128]{2,1,0:T(8,128)S(1)} %get-tuple-element.46, f32[2,16,128]{2,1,0:T(8,128)S(1)} %fusion.45, pred[2,384]{1,0:T(4,128)(4,1)S(1)} %copy-done.10, bf16[2,384,16,64]{1,3,2,0:T(8,128)(2,1)S(1)} %copy-done.6, ...), kind=kOutput, calls=%fused_computation.12 | convolution fusion | flops 212336640 | bytes 11567872 | tf_op jit(solution)/shard_map/bthc,blhc->bhtl/dot_general | solution.py:145
  93.8 3.2 %convolution_bitcast_fusion.1 = f32[2,384,16,64]{1,3,2,0:T(8,128)} fusion(bf16[2,128,16,64]{1,0,3,2:T(2,128)(2,1)S(1)} %copy-done.3, f32[2,16,384,128]{3,2,1,0:T(8,128)S(1)} %get-tuple-element.43, f32[2,16,128]{2,1,0:T(8,128)S(1)} %fusion.45, pred[2,384]{1,0:T(4,128)(4,1)S(1)} %copy-done.10), kind=kOutput, calls=%fused_computation.22 | convolution fusion | flops 207618048 | bytes 9978624 | tf_op jit(solution)/shard_map/bhtl,bthc->blhc/dot_general | solution.py:181
  97.1 0.2 copy.144
  97.2 0.8 stack_reshape.7
  98.0 2.4 %copy.121 = bf16[2,128,16,64]{1,0,3,2:T(2,128)(2,1)} copy(bf16[2,128,16,64]{1,3,2,0:T(8,128)(2,1)} %get-tuple-element.47) | data formatting | bytes 1048576 | tf_op jit(solution)/shard_map/convert_element_type | solution.py:134
  100.4 1.3 fusion.19
  101.7 0.3 convolution_bitcast_fusion.9
  101.9 0.2 copy.142
  102.2 1.6 pad_maximum_fusion.3
  103.9 5.1 %convolution_bitcast_fusion.2 = f32[2,384,16,64]{1,3,2,0:T(8,128)} fusion(bf16[2,16,128,384]{2,3,1,0:T(8,128)(2,1)} %multiply_convert_fusion, bf16[2,128,16,64]{1,0,3,2:T(2,128)(2,1)S(1)} %reshape_reshape.6), kind=kOutput, calls=%fused_computation.23 | convolution fusion | flops 201326592 | bytes 6815744 | tf_op jit(solution)/shard_map/bhtl,bthc->blhc/dot_general | solution.py:178
  109.0 6.1 %copy.134 = f32[2,384,16,64]{3,2,1,0:T(8,128)} copy(f32[2,384,16,64]{1,3,2,0:T(8,128)} %convolution_bitcast_fusion.2) | data formatting | bytes 6291456 | tf_op jit(solution)/shard_map/bhtl,bthc->blhc/transpose | solution.py:178
  115.1 6.7 %stack.49 = f32[1,6,131072]{2,1,0:T(8,128)} reshape(f32[2,384,16,64]{3,2,1,0:T(8,128)} %copy.134) | data formatting | bytes 6291456 | tf_op jit(solution)/shard_map/stack | solution.py:187
  121.8 6.1 %copy.137 = f32[2,384,16,64]{3,2,1,0:T(8,128)} copy(f32[2,384,16,64]{1,3,2,0:T(8,128)} %convolution_bitcast_fusion.1) | data formatting | bytes 6291456 | tf_op jit(solution)/shard_map/bhtl,bthc->blhc/transpose | solution.py:181
  127.9 6.6 %stack.50 = f32[1,6,131072]{2,1,0:T(8,128)} reshape(f32[2,384,16,64]{3,2,1,0:T(8,128)} %copy.137) | data formatting | bytes 6291456 | tf_op jit(solution)/shard_map/stack | solution.py:187
  134.5 11.1 %convolution_bitcast_fusion = f32[2,6,131072]{2,1,0:T(8,128)} fusion(f32[1,6,131072]{2,1,0:T(8,128)} %stack.50, f32[1,6,131072]{2,1,0:T(8,128)} %stack.49, s32[6]{0:T(128)S(1)} %copy-done.15), kind=kOutput, calls=%fused_computation.2 | convolution fusion | flops 114819104 | bytes 12582936 | tf_op jit(solution)/shard_map/ne,xnk->xek/dot_general | solution.py:188
  145.7 7.2 %reshape.89 = f32[2,3,256,1024]{3,2,1,0:T(8,128)} reshape(f32[2,6,131072]{2,1,0:T(8,128)} %convolution_bitcast_fusion) | data formatting | bytes 12582912 | tf_op jit(solution)/shard_map/reshape | solution.py:188
  152.8 3.3 %convert.9 = bf16[2,3,256,1024]{3,2,1,0:T(8,128)(2,1)S(1)} convert(f32[2,3,256,1024]{3,2,1,0:T(8,128)} %reshape.89) | non-fusion elementwise | flops 1572864 | bytes 9437184 | tf_op jit(solution)/shard_map/convert.4
  156.1 1.5 slice_bitcast_fusion.2
  157.6 1.6 collective-permute-start.6
  159.3 0.3 convolution_bitcast_fusion.3
  159.7 1.6 fusion.14
  161.2 1.5 convolution_convert_fusion.1
  162.8 1.8 copy.168
  164.6 1.5 reshape.124
  166.1 27.7 %all-reduce.3.cloned.1.call-done = f32[2,32,1024]{2,1,0:T(8,128)} async-done(((f32[2,32,1024]{2,1,0:T(8,128)}), f32[2,32,1024]{2,1,0:T(8,128)}) %all-reduce.3.cloned.1.call-update) | async-done | bytes 262160
  193.8 0.9 dynamic-slice_divide_fusion
  194.7 2.8 %fusion.10 = bf16[2,256,1024]{2,1,0:T(8,128)(2,1)S(1)} fusion(f32[2,3,256,1024]{3,2,1,0:T(8,128)} %reshape.89, bf16[2,256,1024]{2,1,0:T(8,128)(2,1)} %collective-permute-done.7, bf16[2,256,1024]{2,1,0:T(8,128)(2,1)} %collective-permute-done.6, f32[2,2,1024]{2,1,0:T(2,128)S(1)} %dynamic-slice_divide_fusion, f32[256]{0:T(256)S(1)} %copy-done.13), kind=kLoop, calls=%fused_computation.20 | loop fusion | flops 3670016 | bytes 5260288 | tf_op jit(solution)/shard_map/convert.2
  197.5 1.0 slice_bitcast_fusion.3
  (75 shorter events, 2.3 us)
Async XLA Ops:
  7.2 14.5 %copy-start = (bf16[1024,1024]{1,0:T(8,128)(2,1)S(1)}, bf16[1024,1024]{1,0:T(8,128)(2,1)}, u32[]{:S(2)}) copy-start(bf16[1024,1024]{1,0:T(8,128)(2,1)} %param.11) | copy-start | bytes 6291460
  7.2 14.5 %copy-start.16 = (bf16[256,1024]{1,0:T(8,128)(2,1)S(1)}, bf16[256,1024]{1,0:T(8,128)(2,1)}, u32[]{:S(2)}) copy-start(bf16[256,1024]{1,0:T(8,128)(2,1)} %param.10) | copy-start | bytes 1572868
  7.2 186.6 %all-reduce.3.cloned.1.call-start = ((), (), s32[]{:S(2)}) async-start(), calls=%async_computation | async-start | bytes 524288
  9.7 40.5 %collective-permute-start.1 = (bf16[2,256,1024]{2,1,0:T(8,128)(2,1)}, bf16[2,256,1024]{2,1,0:T(8,128)(2,1)}, u32[]{:S(2)}, u32[]{:S(2)}) collective-permute-start(bf16[2,256,1024]{2,1,0:T(8,128)(2,1)} %pad_maximum_fusion.1), channel_id=1, source_target_pairs={{1,0},{2,1},{3,2},{4,3},{5,4},{6,5},{7,6},{8,7},{9,8},{10,9},{11,1... | collective-permute-start | bytes 3145736 | tf_op jit(solution)/shard_map/ppermute | solution.py:46
  15.1 35.1 %collective-permute-start = (bf16[2,256,1024]{2,1,0:T(8,128)(2,1)}, bf16[2,256,1024]{2,1,0:T(8,128)(2,1)}, u32[]{:S(2)}, u32[]{:S(2)}) collective-permute-start(bf16[2,256,1024]{2,1,0:T(8,128)(2,1)} %pad_maximum_fusion.1), channel_id=1, source_target_pairs={{0,1},{1,2},{2,3},{3,4},{4,5},{5,6},{6,7},{7,8},{8,9},{9,10},{10,1... | collective-permute-start | bytes 3145736 | tf_op jit(solution)/shard_map/ppermute | solution.py:44
  18.4 5.8 %copy-start.11 = (f32[2]{0:T(128)}, f32[2]{0:T(128)S(1)}, u32[]{:S(2)}) copy-start(f32[2]{0:T(128)S(1)} %convert_sqrt_fusion) | copy-start | bytes 28
  21.6 17.4 %copy-start.14 = (s32[32,3]{0,1:T(4,128)S(1)}, s32[32,3]{0,1:T(4,128)}, u32[]{:S(2)}) copy-start(s32[32,3]{0,1:T(4,128)} %param.12) | copy-start | bytes 1156
  21.6 2.7 %collective-permute-start.2 = (bf16[1,2,2,1024]{3,2,0,1:T(2,128)(2,1)S(1)}, bf16[1,2,2,1024]{3,2,0,1:T(2,128)(2,1)S(1)}, u32[]{:S(2)}, u32[]{:S(2)}) collective-permute-start(bf16[1,2,2,1024]{3,2,0,1:T(2,128)(2,1)S(1)} %fusion.47), channel_id=1, source_target_pairs={{0,1},{1,0},{2,3},{3,2},{4,5},{5,4},{6,7},{7,6},{8,9},{9,8},{10,11... | collective-permute-start | bytes 24584 | tf_op jit(solution)/shard_map/ppermute | solution.py:22
  22.4 25.5 %copy-start.17 = (u32[32]{0:T(128)S(1)}, u32[32]{0:T(128)}, u32[]{:S(2)}) copy-start(u32[32]{0:T(128)} %constant.62) | copy-start | bytes 388
  22.8 27.2 %copy-start.2 = (bf16[2,128,16,64]{1,0,3,2:T(2,128)(2,1)}, bf16[2,128,16,64]{1,0,3,2:T(2,128)(2,1)S(1)}, u32[]{:S(2)}) copy-start(bf16[2,128,16,64]{1,0,3,2:T(2,128)(2,1)S(1)} %reshape_reshape.7) | copy-start | bytes 1572868
  24.4 12.9 %collective-permute-start.3 = (bf16[2,2,2,1024]{3,2,0,1:T(2,128)(2,1)S(1)}, bf16[2,2,2,1024]{3,2,0,1:T(2,128)(2,1)S(1)}, u32[]{:S(2)}, u32[]{:S(2)}) collective-permute-start(bf16[2,2,2,1024]{3,2,0,1:T(2,128)(2,1)S(1)} %pad_maximum_fusion.6), channel_id=1, source_target_pairs={{0,2},{1,3},{2,0},{3,1},{4,6},{5,7},{6,4},{7,5},{8,10},{9,11},{10,... | collective-permute-start | bytes 49160 | tf_op jit(solution)/shard_map/ppermute | solution.py:22
  37.3 4.0 %collective-permute-start.4 = (bf16[4,2,2,1024]{3,2,0,1:T(2,128)(2,1)S(1)}, bf16[4,2,2,1024]{3,2,0,1:T(2,128)(2,1)S(1)}, u32[]{:S(2)}, u32[]{:S(2)}) collective-permute-start(bf16[4,2,2,1024]{3,2,0,1:T(2,128)(2,1)S(1)} %pad_maximum_fusion.5), channel_id=1, source_target_pairs={{0,4},{1,5},{2,6},{3,7},{4,0},{5,1},{6,2},{7,3},{8,12},{9,13},{10,... | collective-permute-start | bytes 98312 | tf_op jit(solution)/shard_map/ppermute | solution.py:22
  41.5 7.7 %collective-permute-start.5 = (bf16[8,2,2,1024]{3,2,0,1:T(2,128)(2,1)S(1)}, bf16[8,2,2,1024]{3,2,0,1:T(2,128)(2,1)S(1)}, u32[]{:S(2)}, u32[]{:S(2)}) collective-permute-start(bf16[8,2,2,1024]{3,2,0,1:T(2,128)(2,1)S(1)} %pad_maximum_fusion.4), channel_id=1, source_target_pairs={{0,8},{1,9},{2,10},{3,11},{4,12},{5,13},{6,14},{7,15},{8,0},{9,1},... | collective-permute-start | bytes 196616 | tf_op jit(solution)/shard_map/ppermute | solution.py:22
  44.7 38.8 %copy-start.9 = (pred[2,384]{1,0:T(4,128)(4,1)}, pred[2,384]{1,0:T(4,128)(4,1)S(1)}, u32[]{:S(2)}) copy-start(pred[2,384]{1,0:T(4,128)(4,1)S(1)} %broadcast_in_dim.19) | copy-start | bytes 2308
  49.8 35.6 %copy-start.7 = (bf16[32,16,64]{2,1,0:T(8,128)(2,1)}, bf16[32,16,64]{2,1,0:T(8,128)(2,1)S(1)}, u32[]{:S(2)}) copy-start(bf16[32,16,64]{2,1,0:T(8,128)(2,1)S(1)} %reshape_squeeze.15) | copy-start | bytes 196612
  83.5 1.7 copy-start.3
  85.0 1.4 copy-start.6
  85.0 1.7 copy-start.8
  85.0 1.7 copy-start.10
  127.9 6.6 %copy-start.15 = (s32[6]{0:T(128)S(1)}, s32[6]{0:T(128)}, u32[]{:S(2)}) copy-start(s32[6]{0:T(128)} %eq.35) | copy-start | bytes 76
  156.1 3.5 %copy-start.1 = (bf16[2,384,16,64]{1,3,2,0:T(8,128)(2,1)S(1)}, bf16[2,384,16,64]{1,3,2,0:T(8,128)(2,1)}, u32[]{:S(2)}) copy-start(bf16[2,384,16,64]{1,3,2,0:T(8,128)(2,1)} %reshape_squeeze.13) | copy-start | bytes 4718596
  156.1 3.5 %copy-start.4 = (bf16[2,16,128,384]{2,3,1,0:T(8,128)(2,1)S(1)}, bf16[2,16,128,384]{2,3,1,0:T(8,128)(2,1)}, u32[]{:S(2)}) copy-start(bf16[2,16,128,384]{2,3,1,0:T(8,128)(2,1)} %multiply_convert_fusion) | copy-start | bytes 9437188
  157.6 37.1 %collective-permute-start.6 = (bf16[2,256,1024]{2,1,0:T(8,128)(2,1)}, bf16[2,256,1024]{2,1,0:T(8,128)(2,1)}, u32[]{:S(2)}, u32[]{:S(2)}) collective-permute-start(bf16[2,256,1024]{2,1,0:T(8,128)(2,1)} %get-tuple-element.18), channel_id=1, source_target_pairs={{1,0},{2,1},{3,2},{4,3},{5,4},{6,5},{7,6},{8,7},{9,8},{10,9},{11,1... | collective-permute-start | bytes 3145736 | tf_op jit(solution)/shard_map/ppermute | solution.py:56
  159.3 35.4 %collective-permute-start.7 = (bf16[2,256,1024]{2,1,0:T(8,128)(2,1)}, bf16[2,256,1024]{2,1,0:T(8,128)(2,1)}, u32[]{:S(2)}, u32[]{:S(2)}) collective-permute-start(bf16[2,256,1024]{2,1,0:T(8,128)(2,1)} %get-tuple-element.19), channel_id=1, source_target_pairs={{15,0},{0,1},{1,2},{2,3},{3,4},{4,5},{5,6},{6,7},{7,8},{8,9},{9,10... | collective-permute-start | bytes 3145736 | tf_op jit(solution)/shard_map/ppermute | solution.py:56
  159.6 1.6 copy-start.5
  161.2 32.6 %copy-start.12 = (f32[2]{0:T(128)S(1)}, f32[2]{0:T(128)}, u32[]{:S(2)}) copy-start(f32[2]{0:T(128)} %copy-done.11) | copy-start | bytes 28
  161.2 33.5 %copy-start.13 = (f32[256]{0:T(256)S(1)}, f32[256]{0:T(256)}, u32[]{:S(2)}) copy-start(f32[256]{0:T(256)} %get-tuple-element.34) | copy-start | bytes 3076
Sparse Core Ops, SparseCore 0:
  104.0 89.7 all-reduce.2
